TPU v7x, 1024 devices: a whole 4x8x16 slice. The times are simulated.
1024 devices in a mesh: dp: 16 (over y, core), expert: 16 (over z), head: 4 (over x).
Axes of the slice: x: 4, y: 8, z: 16, core: 2. Of those that a mesh axis runs over, the one named last changes fastest.
Arguments:
- tokens: bfloat16 [32768, 4096], P(('dp', 'expert')), may hold values from -6 to 6
- routes: int32 [32768, 8], P(('dp', 'expert')), may hold values from 0 to 127, all different within a row; in each aligned block of 128 rows (0 to 127, 128 to 255, ...) at most 16 rows name the same one
- route_weights: float32 [32768, 8], P(('dp', 'expert')), may hold values from 0.05 to 1
- gate_weight: bfloat16 [16, 4096, 1024], P('expert', None, 'head'), may hold values from -0.09375 to 0.09375
- up_weight: bfloat16 [16, 4096, 1024], P('expert', None, 'head'), may hold values from -0.09375 to 0.09375
- down_weight: bfloat16 [16, 1024, 4096], P('expert', 'head', 'dp'), may hold values from -0.1875 to 0.1875
Outputs:
- combined: bfloat16 [32768, 4096], P(('dp', 'expert'), 'head')
Inputs may be any that keep to these rules, and one draw needn't show every extreme that they name: `routes`: each row names 8 different experts; among the 128 rows of one device, no expert is named by more than 16 rows, a bound that some block reaches.
All inputs are finite; a program needn't handle non-finite values.
Results may differ from a plain program's by a relative error of at most 0.017.
Values may be sent and summed in bfloat16 or wider, within the bound.
A program may use at most 64 MiB of HBM per device.

v0:
```python
import jax
import jax.numpy as jnp
from jax import lax
from jax.sharding import PartitionSpec as P

EXPERTS = 128


def body(tokens, routes, route_weights, gate_weight, up_weight, down_weight):
    groups = lax.axis_size("expert")
    tok_rows, model_width = tokens.shape
    capacity = tok_rows // 8
    local_experts = EXPERTS // groups
    targets = jnp.arange(groups, dtype=jnp.int32) * local_experts
    matches = routes[:, :, None] == targets[None, None, :]
    chosen = jnp.any(matches, axis=1)
    weight = jnp.sum(jnp.where(matches, route_weights[:, :, None], 0.0), axis=1)
    position = jnp.cumsum(chosen.astype(jnp.int32), axis=0) - 1
    slot_ids = jnp.arange(capacity, dtype=jnp.int32)
    picker = chosen.T[:, None, :] & (position.T[:, None, :] == slot_ids[None, :, None])
    picker_half = picker.astype(jnp.bfloat16)
    outgoing = jnp.einsum(
        "gct,tf->gcf", picker_half, tokens, preferred_element_type=jnp.float32
    ).astype(jnp.bfloat16)
    arrived = lax.all_to_all(outgoing, "expert", split_axis=0, concat_axis=0, tiled=True)
    slot_rows = arrived.reshape(groups * capacity, model_width)
    gate_act = jnp.dot(slot_rows, gate_weight[0], preferred_element_type=jnp.float32)
    up_act = jnp.dot(slot_rows, up_weight[0], preferred_element_type=jnp.float32)
    hidden = (jax.nn.silu(gate_act) * up_act).astype(jnp.bfloat16)
    partial_value = jnp.dot(
        hidden,
        lax.all_gather(down_weight[0], "dp", axis=1, tiled=True),
        preferred_element_type=jnp.float32,
    )
    rounded = partial_value.astype(jnp.bfloat16).astype(jnp.float32)
    summed = lax.psum_scatter(
        rounded.reshape(groups, capacity, model_width).astype(jnp.bfloat16),
        "head",
        scatter_dimension=2,
        tiled=True,
    )
    returned = lax.all_to_all(summed, "expert", split_axis=0, concat_axis=0, tiled=True)
    mixing = picker.astype(jnp.float32) * weight.T[:, None, :]
    combined = jnp.einsum("gct,gcf->tf", mixing, returned.astype(jnp.float32))
    return combined.astype(jnp.bfloat16)


def solution(mesh):
    return jax.shard_map(
        body,
        mesh=mesh,
        in_specs=(
            P(("dp", "expert"), None),
            P(("dp", "expert"), None),
            P(("dp", "expert"), None),
            P("expert", None, "head"),
            P("expert", None, "head"),
            P("expert", "head", "dp"),
        ),
        out_specs=P(("dp", "expert"), "head"),
        check_vma=False,
    )
```

profile of v0, /device:TPU:24, one launch (start us, length us, event | category | flops | bytes accessed | tf_op | source)
XLA Modules:
  0.0 221.1 jit_solution(5841387241895303934)
XLA Ops:
  6.5 0.0 copy-start
  6.5 0.9 compare_reduce_fusion
  7.5 0.1 copy.19
  7.6 0.2 reduce_window_sum.11
  7.7 0.1 copy.20
  7.9 3.2 %convolution_convert_fusion = bf16[16,16,4096]{2,1,0:T(8,128)(2,1)} fusion(bf16[128,4096]{1,0:T(8,128)(2,1)} %param.6, pred[16,16,128]{2,0,1:T(8,128)(4,1)S(1)} %fusion.23), kind=kOutput, calls=%fused_computation | convolution fusion | flops 269484032 | bytes 3178496 | tf_op jit(solution)/shard_map/gct,tf->gcf/dot_general | solution.py:22
  11.1 18.9 %all-to-all-start = ((bf16[16,16,4096]{2,1,0:T(8,128)(2,1)}), bf16[16,16,4096]{2,1,0:T(8,128)(2,1)}, u32[]{:S(2)}, u32[]{:S(2)}) async-start(bf16[16,16,4096]{2,1,0:T(8,128)(2,1)} %convolution_convert_fusion), calls=%async_computation | async-start | bytes 4194304 | tf_op jit(solution)/shard_map/all_to_all | solution.py:25
  30.0 0.0 all-gather.3.cloned.1.call-start
  30.1 0.7 all-gather.3.cloned.1.call-update
  30.8 0.0 reduce-scatter.2.cloned.1.call-start
  30.8 94.9 %all-to-all-done = bf16[16,16,4096]{2,1,0:T(8,128)(2,1)} async-done(((bf16[16,16,4096]{2,1,0:T(8,128)(2,1)}), bf16[16,16,4096]{2,1,0:T(8,128)(2,1)}, u32[]{:S(2)}, u32[]{:S(2)}) %all-to-all-start) | async-done | bytes 2097184 | tf_op jit(solution)/shard_map/all_to_all | solution.py:25
  125.7 2.9 %fusion.3 = f32[256,256]{1,0:T(8,128)S(1)} fusion(bf16[256,4096]{1,0:T(8,128)(2,1)} %bitcast.4, bf16[1,4096,256]{2,1,0:T(8,128)(2,1)} %param.9), kind=kOutput, calls=%fused_computation.5 | convolution fusion | flops 536870912 | bytes 4456448 | tf_op jit(solution)/shard_map/dot_general | solution.py:27
  128.6 0.0 all-gather.3.cloned.1.call-done
  128.6 0.0 copy-done
  128.7 5.9 %convolution_convert_fusion.1 = bf16[256,4096]{1,0:T(8,128)(2,1)} fusion(bf16[1,256,4096]{2,1,0:T(8,128)(2,1)} %all-gather.3.cloned.1.call-done, bf16[256,4096]{1,0:T(8,128)(2,1)} %bitcast.4, bf16[1,4096,256]{2,1,0:T(8,128)(2,1)S(1)} %copy-done, f32[256,256]{1,0:T(8,128)S(1)} %fusion.3), kind=kOutput, calls=%fused_computation.1 | convolution fusion | flops 1075183616 | bytes 8650752 | tf_op jit(solution)/shard_map/dot_general | solution.py:30
  134.6 0.0 copy-start.1
  134.6 0.0 copy-start.2
  134.6 0.0 reduce-scatter.2.cloned.1.call-update
  134.6 36.3 %reduce-scatter.2.cloned.1.call-done = bf16[16,16,1024]{2,1,0:T(8,128)(2,1)} async-done(((bf16[16,16,4096]{2,1,0:T(8,128)(2,1)}), bf16[16,16,1024]{2,1,0:T(8,128)(2,1)}) %reduce-scatter.2.cloned.1.call-update) | async-done | bytes 524304 | tf_op jit(solution)/shard_map/reduce_scatter | solution.py:36
  170.9 13.0 %all-to-all-start.1 = ((bf16[16,16,1024]{2,1,0:T(8,128)(2,1)}), bf16[16,16,1024]{2,1,0:T(8,128)(2,1)S(1)}, u32[]{:S(2)}, u32[]{:S(2)}) async-start(bf16[16,16,1024]{2,1,0:T(8,128)(2,1)} %reduce-scatter.2.cloned.1.call-done), calls=%async_computation.2 | async-start | bytes 1048576 | tf_op jit(solution)/shard_map/all_to_all | solution.py:42
  183.9 0.0 copy-done.1
  184.0 0.0 copy-done.2
  184.0 0.1 fusion.25
  184.0 29.0 %all-to-all-done.1 = bf16[16,16,1024]{2,1,0:T(8,128)(2,1)S(1)} async-done(((bf16[16,16,1024]{2,1,0:T(8,128)(2,1)}), bf16[16,16,1024]{2,1,0:T(8,128)(2,1)S(1)}, u32[]{:S(2)}, u32[]{:S(2)}) %all-to-all-start.1) | async-done | bytes 524320 | tf_op jit(solution)/shard_map/all_to_all | solution.py:42
  213.1 1.2 fusion.5
  (4 shorter events, 0.1 us)
Async XLA Ops:
  6.5 122.1 %copy-start = (bf16[1,4096,256]{2,1,0:T(8,128)(2,1)S(1)}, bf16[1,4096,256]{2,1,0:T(8,128)(2,1)}, u32[]{:S(2)}) copy-start(bf16[1,4096,256]{2,1,0:T(8,128)(2,1)} %param.10) | copy-start | bytes 6291460
  11.1 114.6 %all-to-all-start = ((bf16[16,16,4096]{2,1,0:T(8,128)(2,1)}), bf16[16,16,4096]{2,1,0:T(8,128)(2,1)}, u32[]{:S(2)}, u32[]{:S(2)}) async-start(bf16[16,16,4096]{2,1,0:T(8,128)(2,1)} %convolution_convert_fusion), calls=%async_computation | async-start | bytes 4194304 | tf_op jit(solution)/shard_map/all_to_all | solution.py:25
  30.0 98.6 %all-gather.3.cloned.1.call-start = ((), (), s32[]{:S(2)}) async-start(), calls=%async_computation.4 | async-start | bytes 2228224 | tf_op jit(solution)/shard_map/all_gather | solution.py:32
  30.8 140.2 %reduce-scatter.2.cloned.1.call-start = ((), (), s32[]{:S(2)}) async-start(), calls=%async_computation.3 | async-start | bytes 2621440 | tf_op jit(solution)/shard_map/reduce_scatter | solution.py:36
  134.6 49.4 %copy-start.1 = (s32[128,8]{0,1:T(8,128)S(1)}, s32[128,8]{0,1:T(8,128)}, u32[]{:S(2)}) copy-start(s32[128,8]{0,1:T(8,128)} %param.7) | copy-start | bytes 12292
  134.6 49.4 %copy-start.2 = (f32[128,8]{0,1:T(8,128)S(1)}, f32[128,8]{0,1:T(8,128)}, u32[]{:S(2)}) copy-start(f32[128,8]{0,1:T(8,128)} %param.8) | copy-start | bytes 12292
  170.9 42.1 %all-to-all-start.1 = ((bf16[16,16,1024]{2,1,0:T(8,128)(2,1)}), bf16[16,16,1024]{2,1,0:T(8,128)(2,1)S(1)}, u32[]{:S(2)}, u32[]{:S(2)}) async-start(bf16[16,16,1024]{2,1,0:T(8,128)(2,1)} %reduce-scatter.2.cloned.1.call-done), calls=%async_computation.2 | async-start | bytes 1048576 | tf_op jit(solution)/shard_map/all_to_all | solution.py:42
Sparse Core Ops, SparseCore 0:
  33.5 48.8 all-gather.2
  134.7 36.1 reduce-scatter.1
where the time goes:
time: 222 us; the launch traced here: 221 us
  waiting for transfers between devices  161 us (73%)
  starting transfers between devices  32 us (14%)
  between operations  13.5 us (6%)
  matrix products  13.3 us (6%)
    all_to_all x1, waiting for transfers between devices, body(): lax.all_to_all(outgoing, 'expert', split_axis=0, concat_axis=0, tiled=True)  94.9 us
    reduce_scatter x1, waiting for transfers between devices, body(): lax.psum_scatter(rounded.reshape(groups, capacity, model_width).astype(jn...  36.3 us
    all_to_all x1, waiting for transfers between devices, body(): lax.all_to_all(summed, 'expert', split_axis=0, concat_axis=0, tiled=True)  29 us
    all_to_all x1, starting transfers between devices, body(): lax.all_to_all(outgoing, 'expert', split_axis=0, concat_axis=0, tiled=True)  18.9 us
    all_to_all x1, starting transfers between devices, body(): lax.all_to_all(summed, 'expert', split_axis=0, concat_axis=0, tiled=True)  13 us
    dot_general x1, matrix products, body(): jnp.dot(hidden, lax.all_gather(down_weight[0], 'dp', axis=1, tiled=True),...  5.92 us
  transfers between devices with their start and end apart: 4, of which 3 were waited for; matrix products, arithmetic and copies ran while one was open for 1% of the time, Pallas kernels for 0%

commit v1 on v0

v1 whole, which is shorter than its diff:
```python
import jax
import jax.numpy as jnp
from jax import lax
from jax.experimental import pallas as pl
from jax.experimental.pallas import tpu as pltpu
from jax.sharding import PartitionSpec as P

MESH = pl.DeviceIdType.MESH
CAP = 16
NZ = 16
NY = 8
NX = 4
QUARTER = 1024
ROWS = NZ * CAP
GROUPS = ((0, 5), (5, 11), (11, 16))
Y_OFFSETS = (1, -1, 2, -2, 3, -3, 4)


def offset_of(k):
    size = 8 - (k + 1) // 2
    return size * (2 * (k % 2) - 1)


def y_index(off):
    return Y_OFFSETS.index((off + 3) % NY - 3)


def rows_of(k):
    return pl.ds(pl.multiple_of(k * CAP, CAP), CAP)


def kernel(
    tokens, routes, route_weights, gate, up, down,
    out,
    tok, rts, rtw, wg, wu, dn, outbox, arr, hid, part, relay_out, relay_in, sums_out, sums_in, summed, ret,
    load_sem, zs, zr, xs, xr, ys, yr, cs, cr, ls, lr, ss, sr, bs, br,
):
    dp = lax.axis_index("dp")
    y, core = dp // 2, dp % 2
    e = lax.axis_index("expert")
    h = lax.axis_index("head")

    def z_peer(off):
        return {"expert": (e + off + 2 * NZ) % NZ}

    def x_peer(off):
        return {"head": (h + off + NX) % NX}

    def y_dp(off):
        return ((y + off + NY) % NY) * 2 + core

    sibling = y * 2 + (1 - core)

    loads = [
        pltpu.make_async_copy(routes, rts, load_sem.at[0]),
        pltpu.make_async_copy(route_weights, rtw, load_sem.at[1]),
        pltpu.make_async_copy(
            tokens.at[:, pl.ds(pl.multiple_of(h * QUARTER, QUARTER), QUARTER)], tok, load_sem.at[2]
        ),
        pltpu.make_async_copy(down.at[0], dn.at[dp], load_sem.at[3]),
    ]
    for r, off in enumerate((0, -1, 1, 2)):
        q = (h + off + NX) % NX
        src = pl.ds(pl.multiple_of(q * QUARTER, QUARTER), QUARTER)
        loads.append(pltpu.make_async_copy(gate.at[0, src], wg.at[r], load_sem.at[4 + 2 * r]))
        loads.append(pltpu.make_async_copy(up.at[0, src], wu.at[r], load_sem.at[5 + 2 * r]))
    for copy in loads:
        copy.start()

    bar = pltpu.get_barrier_semaphore()

    def greet(i, c):
        pl.semaphore_signal(bar, inc=1, device_id=z_peer(i), device_id_type=MESH)
        return c

    lax.fori_loop(1, NZ, greet, 0)
    for off in (1, -1, 2):
        pl.semaphore_signal(bar, inc=1, device_id=x_peer(off), device_id_type=MESH)
    for off in (1, -1, 2, -2):
        pl.semaphore_signal(bar, inc=1, device_id={"dp": y_dp(off)}, device_id_type=MESH)
    pl.semaphore_signal(bar, inc=1, device_id={"dp": sibling}, device_id_type=MESH)

    tok_rows = tok.shape[0]
    col = lax.broadcasted_iota(jnp.int32, (tok_rows, ROWS), 1)
    block = col >> 4
    slot = col & (CAP - 1)
    size = 8 - ((block + 1) >> 1)
    target = ((e + NZ + jnp.where((block & 1) == 1, size, -size)) & (NZ - 1)) * 8
    loads[0].wait()
    loads[1].wait()
    chosen = jnp.zeros((tok_rows, ROWS), jnp.float32)
    weight = jnp.zeros((tok_rows, ROWS), jnp.float32)
    for i in range(8):
        match = rts[:, i : i + 1] == target
        chosen = jnp.where(match, 1.0, chosen)
        weight = jnp.where(match, rtw[:, i : i + 1], weight)
    earlier = (
        lax.broadcasted_iota(jnp.int32, (tok_rows, tok_rows), 0)
        >= lax.broadcasted_iota(jnp.int32, (tok_rows, tok_rows), 1)
    )
    count = jnp.dot(
        jnp.where(earlier, 1.0, 0.0).astype(jnp.bfloat16),
        chosen.astype(jnp.bfloat16),
        preferred_element_type=jnp.float32,
    )
    picked = jnp.where(count == (slot + 1).astype(jnp.float32), chosen, 0.0)
    mix = picked * weight
    mix_high = mix.astype(jnp.bfloat16)
    mix_low = (mix - mix_high.astype(jnp.float32)).astype(jnp.bfloat16)
    loads[2].wait()
    outbox[...] = lax.dot_general(
        picked.astype(jnp.bfloat16), tok[...], (((0,), (0,)), ((), ())), preferred_element_type=jnp.float32
    ).astype(jnp.bfloat16)
    loads[3].wait()

    pl.semaphore_wait(bar, (NZ - 1) + 3 + 4 + 1)

    def y_copy(block_off, to_off):
        there = y_index(block_off - to_off)
        return pltpu.make_async_remote_copy(
            src_ref=dn.at[y_dp(block_off)],
            dst_ref=dn.at[y_dp(block_off)],
            send_sem=ys.at[there],
            recv_sem=yr.at[there],
            device_id={"dp": y_dp(to_off)},
            device_id_type=MESH,
        )

    def y_arrived(off):
        pltpu.make_async_remote_copy(
            src_ref=dn.at[y_dp(off)],
            dst_ref=dn.at[y_dp(off)],
            send_sem=ys.at[y_index(off)],
            recv_sem=yr.at[y_index(off)],
            device_id={"dp": y_dp(off)},
            device_id_type=MESH,
        ).wait_recv()

    def core_copy(off):
        i = (off + NY) % NY
        return pltpu.make_async_remote_copy(
            src_ref=dn.at[y_dp(off)],
            dst_ref=dn.at[y_dp(off)],
            send_sem=cs.at[i],
            recv_sem=cr.at[i],
            device_id={"dp": sibling},
            device_id_type=MESH,
        )

    def core_arrived(off):
        i = (off + NY) % NY
        there = ((y + off + NY) % NY) * 2 + (1 - core)
        pltpu.make_async_remote_copy(
            src_ref=dn.at[there],
            dst_ref=dn.at[there],
            send_sem=cs.at[i],
            recv_sem=cr.at[i],
            device_id={"dp": sibling},
            device_id_type=MESH,
        ).wait_recv()

    def z_copy(k):
        return pltpu.make_async_remote_copy(
            src_ref=outbox.at[rows_of(k)],
            dst_ref=arr.at[0, rows_of(k)],
            send_sem=zs.at[k],
            recv_sem=zr.at[k],
            device_id=z_peer(offset_of(k)),
            device_id_type=MESH,
        )

    def x_copy(j, off, k):
        return pltpu.make_async_remote_copy(
            src_ref=arr.at[0, rows_of(k)],
            dst_ref=arr.at[j + 1, rows_of(k)],
            send_sem=xs.at[j, k],
            recv_sem=xr.at[j, k],
            device_id=x_peer(off),
            device_id_type=MESH,
        )

    def back_copy(k):
        return pltpu.make_async_remote_copy(
            src_ref=summed.at[rows_of(k)],
            dst_ref=ret.at[rows_of(k)],
            send_sem=bs.at[k],
            recv_sem=br.at[k],
            device_id=z_peer(-offset_of(k)),
            device_id_type=MESH,
        )

    def loop(lo, hi, step):
        def run(k, c):
            step(k)
            return c

        lax.fori_loop(lo, hi, run, 0)

    def spread(k):
        for j, off in enumerate((1, -1, 2)):
            x_copy(j, off, k).start()

    def pass_on(k):
        z_copy(k).wait_recv()
        spread(k)

    y_first = [y_copy(0, off) for off in (1, -1, 2, -2)]
    loop(0, NZ - 1, lambda k: z_copy(k).start())
    for copy in y_first:
        copy.start()
    core_copy(0).start()
    arr[0, (NZ - 1) * CAP :, :] = outbox[(NZ - 1) * CAP :, :]
    spread(NZ - 1)

    loop(0, 3, pass_on)
    y_arrived(-2)
    y_arrived(2)
    y_second = [y_copy(-2, 1), y_copy(-2, 2), y_copy(2, -1)]
    for copy in y_second:
        copy.start()
    y_arrived(-1)
    y_arrived(1)
    for off in (-1, 1, -2, 2):
        core_copy(off).start()
    for copy in loads[4:]:
        copy.wait()
    loop(3, 7, pass_on)

    def expert_front(first, last):
        n = (last - first) * CAP
        rows = slice(first * CAP, last * CAP)
        gate_act = jnp.zeros((n, wg.shape[2]), jnp.float32)
        up_act = jnp.zeros((n, wg.shape[2]), jnp.float32)
        for r in range(NX):
            if r:
                off = (1, -1, 2)[r - 1]
                loop(first, last, lambda k: x_copy(r - 1, off, k).wait_recv())
            a = arr[r, rows, :]
            gate_act += jnp.dot(a, wg[r], preferred_element_type=jnp.float32)
            up_act += jnp.dot(a, wu[r], preferred_element_type=jnp.float32)
        hidden = gate_act / (1.0 + jnp.exp(-gate_act)) * up_act
        hid[rows, :] = hidden.astype(jnp.bfloat16)

    def relay_copy(g, side):
        first, last = GROUPS[g]
        middle = (first + last) // 2
        lo, hi = (first, middle) if side == 0 else (middle, last)
        rows = pl.ds(lo * CAP, (hi - lo) * CAP)
        return pltpu.make_async_remote_copy(
            src_ref=relay_out.at[rows],
            dst_ref=relay_in.at[rows],
            send_sem=ls.at[g, side],
            recv_sem=lr.at[g, side],
            device_id=x_peer(1 - 2 * side),
            device_id_type=MESH,
        )

    def sums_copy(g, side):
        first, last = GROUPS[g]
        rows = pl.ds(first * CAP, (last - first) * CAP)
        return pltpu.make_async_remote_copy(
            src_ref=sums_out.at[side, rows],
            dst_ref=sums_in.at[side, rows],
            send_sem=ss.at[g, side],
            recv_sem=sr.at[g, side],
            device_id=x_peer(1 - 2 * side),
            device_id_type=MESH,
        )

    def expert_back(g):
        first, last = GROUPS[g]
        rows = slice(first * CAP, last * CAP)
        hidden = hid[rows, :]
        for r, off in ((3, 2), (1, 1), (2, -1), (0, 0)):
            q = (h + off + NX) % NX
            for b in range(4):
                value = jnp.dot(hidden, dn[q * 4 + b], preferred_element_type=jnp.float32)
                cols = slice(b * 256, (b + 1) * 256)
                if r == 3:
                    relay_out[rows, cols] = value.astype(jnp.bfloat16)
                else:
                    part[r, rows, cols] = value
            if r == 3:
                relay_copy(g, 0).start()
                relay_copy(g, 1).start()

    def relay(g):
        first, last = GROUPS[g]
        middle = (first + last) // 2
        for side in range(2):
            relay_copy(g, side).wait_recv()
            lo, hi = (first, middle) if side == 0 else (middle, last)
            through = slice(lo * CAP, hi * CAP)
            own = slice(middle * CAP, last * CAP) if side == 0 else slice(first * CAP, middle * CAP)
            sums_out[side, own, :] = part[1 + side, own, :].astype(jnp.bfloat16)
            sums_out[side, through, :] = (
                part[1 + side, through, :] + relay_in[through, :].astype(jnp.float32)
            ).astype(jnp.bfloat16)
            sums_copy(g, side).start()

    def finish(g):
        first, last = GROUPS[g]
        rows = slice(first * CAP, last * CAP)
        sums_copy(g, 0).wait_recv()
        sums_copy(g, 1).wait_recv()
        summed[rows, :] = (
            part[0, rows, :]
            + sums_in[0, rows, :].astype(jnp.float32)
            + sums_in[1, rows, :].astype(jnp.float32)
        ).astype(jnp.bfloat16)
        loop(first, min(last, NZ - 1), lambda k: back_copy(k).start())

    expert_front(*GROUPS[0])
    for off in (-3, 3, 4):
        y_arrived(off)
        core_copy(off).start()
    for i in range(NY):
        core_arrived(i)
    expert_back(0)
    loop(7, 11, pass_on)
    relay(0)
    loop(11, NZ - 1, pass_on)
    expert_front(*GROUPS[1])
    expert_back(1)
    finish(0)
    relay(1)
    expert_front(*GROUPS[2])
    expert_back(2)
    finish(1)
    relay(2)
    finish(2)
    ret[(NZ - 1) * CAP :, :] = summed[(NZ - 1) * CAP :, :]

    loop(0, NZ - 1, lambda k: z_copy(k).wait_send())
    for j, off in enumerate((1, -1, 2)):
        loop(0, NZ, lambda k: x_copy(j, off, k).wait_send())
    for copy in y_first + y_second:
        copy.wait_send()
    for i in range(NY):
        core_copy(i).wait_send()
    for g in range(len(GROUPS)):
        for side in range(2):
            relay_copy(g, side).wait_send()
            sums_copy(g, side).wait_send()
    loop(0, NZ - 1, lambda k: back_copy(k).wait_send())

    loop(0, NZ - 1, lambda k: back_copy(k).wait_recv())
    combined = jnp.dot(mix_high, ret[...], preferred_element_type=jnp.float32)
    combined += jnp.dot(mix_low, ret[...], preferred_element_type=jnp.float32)
    out[...] = combined.astype(jnp.bfloat16)


def body(tokens, routes, route_weights, gate_weight, up_weight, down_weight):
    tok_rows = tokens.shape[0]
    hidden = gate_weight.shape[2]
    bf16, f32 = jnp.bfloat16, jnp.float32
    dma = pltpu.SemaphoreType.DMA
    groups = len(GROUPS)
    return pl.pallas_call(
        kernel,
        out_shape=jax.ShapeDtypeStruct((tok_rows, QUARTER), bf16),
        in_specs=[pl.BlockSpec(memory_space=pl.ANY)] * 6,
        out_specs=pl.BlockSpec(memory_space=pltpu.VMEM),
        scratch_shapes=[
            pltpu.VMEM((tok_rows, QUARTER), bf16),
            pltpu.VMEM((tok_rows, 8), jnp.int32),
            pltpu.VMEM((tok_rows, 8), f32),
            pltpu.VMEM((NX, QUARTER, hidden), bf16),
            pltpu.VMEM((NX, QUARTER, hidden), bf16),
            pltpu.VMEM((2 * NY, hidden, 256), bf16),
            pltpu.VMEM((ROWS, QUARTER), bf16),
            pltpu.VMEM((NX, ROWS, QUARTER), bf16),
            pltpu.VMEM((ROWS, hidden), bf16),
            pltpu.VMEM((3, ROWS, QUARTER), f32),
            pltpu.VMEM((ROWS, QUARTER), bf16),
            pltpu.VMEM((ROWS, QUARTER), bf16),
            pltpu.VMEM((2, ROWS, QUARTER), bf16),
            pltpu.VMEM((2, ROWS, QUARTER), bf16),
            pltpu.VMEM((ROWS, QUARTER), bf16),
            pltpu.VMEM((ROWS, QUARTER), bf16),
            dma((12,)),
            dma((NZ,)), dma((NZ,)),
            dma((3, NZ)), dma((3, NZ)),
            dma((7,)), dma((7,)),
            dma((NY,)), dma((NY,)),
            dma((groups, 2)), dma((groups, 2)),
            dma((groups, 2)), dma((groups, 2)),
            dma((NZ,)), dma((NZ,)),
        ],
        compiler_params=pltpu.CompilerParams(
            collective_id=0, has_side_effects=True, vmem_limit_bytes=48 * 2**20
        ),
        cost_estimate=pl.CostEstimate(
            flops=2 * ROWS * hidden * 3 * 4096, bytes_accessed=6 * 2**20, transcendentals=ROWS * hidden
        ),
    )(tokens, routes, route_weights, gate_weight, up_weight, down_weight)


def solution(mesh):
    return jax.shard_map(
        body,
        mesh=mesh,
        in_specs=(
            P(("dp", "expert"), None),
            P(("dp", "expert"), None),
            P(("dp", "expert"), None),
            P("expert", None, "head"),
            P("expert", None, "head"),
            P("expert", "head", "dp"),
        ),
        out_specs=P(("dp", "expert"), "head"),
        check_vma=False,
    )
```

time: 222 us -> 101 us (0.45)
  the two profiles are of different devices: /device:TPU:24 before, /device:TPU:1 now
where the time goes in v1:
time: 101 us
  Pallas kernels  93.1 us (92%)
  local copies, waits for them, and re-layouts  7.58 us (8%)
    pallas_call x1, Pallas kernels, body(): pl.pallas_call(kernel, out_shape=jax.ShapeDtypeStruct((tok_rows, QUARTER)...  93.1 us
    unnamed x11, local copies, waits for them, and re-layouts  7.58 us

profile of v1, /device:TPU:1, one launch (start us, length us, event | category | flops | bytes accessed | tf_op | source)
XLA Modules:
  0.0 100.7 jit_solution(13750264780703346711)
XLA Ops:
  0.0 0.8 copy.7.routes
  0.8 0.8 copy.8.route_weights
  1.6 0.0 copy-start
  1.6 1.6 %copy-done = bf16[1,4096,256]{2,1,0:T(8,128)(2,1)S(1)} copy-done((bf16[1,4096,256]{2,1,0:T(8,128)(2,1)S(1)}, bf16[1,4096,256]{2,1,0:T(8,128)(2,1)}, u32[]{:S(2)}) %copy-start) | copy-done | bytes 2097176
  3.2 0.0 copy-start.1
  3.2 1.6 %copy-done.1 = bf16[1,4096,256]{2,1,0:T(8,128)(2,1)S(1)} copy-done((bf16[1,4096,256]{2,1,0:T(8,128)(2,1)S(1)}, bf16[1,4096,256]{2,1,0:T(8,128)(2,1)}, u32[]{:S(2)}) %copy-start.1) | copy-done | bytes 2097176
  4.8 0.0 copy-start.2
  4.8 1.2 %copy-done.2 = bf16[128,4096]{1,0:T(8,128)(2,1)S(1)} copy-done((bf16[128,4096]{1,0:T(8,128)(2,1)S(1)}, bf16[128,4096]{1,0:T(8,128)(2,1)}, u32[]{:S(2)}) %copy-start.2) | copy-done | bytes 1048600
  6.0 0.0 copy-start.3
  6.0 0.9 copy-done.3
  6.9 93.1 %shard_map.64 = bf16[128,1024]{1,0:T(8,128)(2,1)S(1)} custom-call(bf16[128,4096]{1,0:T(8,128)(2,1)S(1)} %copy-done.2, s32[128,8]{1,0:T(8,128)S(1)} %copy.7.routes, f32[128,8]{1,0:T(8,128)S(1)} %copy.8.route_weights, bf16[1,4096,256]{2,1,0:T(8,128)(2,1)S(1)} %copy-done, bf16[1,4096,256]{2,1,0:T(8,128)(2,1)S(1)} %copy-done.1, bf16[1,256,256]{2,1,0:T(8,128)(2,1)S(1)} %copy-done.3), custom_call_target="tpu_custom_call" | custom-call | flops 1610612736 | bytes 6291456 | tf_op jit(solution)/shard_map/pallas_call | solution.py:359
  100.0 0.7 copy.10
Async XLA Ops:
  1.6 1.6 %copy-start = (bf16[1,4096,256]{2,1,0:T(8,128)(2,1)S(1)}, bf16[1,4096,256]{2,1,0:T(8,128)(2,1)}, u32[]{:S(2)}) copy-start(bf16[1,4096,256]{2,1,0:T(8,128)(2,1)} %gate.1) | copy-start | bytes 6291460
  3.2 1.6 %copy-start.1 = (bf16[1,4096,256]{2,1,0:T(8,128)(2,1)S(1)}, bf16[1,4096,256]{2,1,0:T(8,128)(2,1)}, u32[]{:S(2)}) copy-start(bf16[1,4096,256]{2,1,0:T(8,128)(2,1)} %up.1) | copy-start | bytes 6291460
  4.8 1.2 %copy-start.2 = (bf16[128,4096]{1,0:T(8,128)(2,1)S(1)}, bf16[128,4096]{1,0:T(8,128)(2,1)}, u32[]{:S(2)}) copy-start(bf16[128,4096]{1,0:T(8,128)(2,1)} %tokens.1) | copy-start | bytes 3145732
  6.0 0.9 copy-start.3

commit v2 on v1

v2 whole, which is shorter than its diff:
```python
import jax
import jax.numpy as jnp
from jax import lax
from jax.experimental import pallas as pl
from jax.experimental.pallas import tpu as pltpu
from jax.sharding import PartitionSpec as P

MESH = pl.DeviceIdType.MESH
CAP = 16
NZ = 16
NY = 8
NX = 4
QUARTER = 1024
ROWS = NZ * CAP
FRAG = 32
DIRECT = 13
GROUPS = ((0, 5), (5, 9), (9, 13), (13, 16))
Y_OFFSETS = (1, -1, 2, -2, 3, -3, 4)


def offset_of(k):
    return (k + 1) // 2 * (2 * (k % 2) - 1)


def y_index(off):
    return Y_OFFSETS.index((off + 3) % NY - 3)


def rows_of(k):
    return pl.ds(pl.multiple_of(k * CAP, CAP), CAP)


def kernel(
    tokens, routes, route_weights, gate, up, down,
    out,
    tok, rts, rtw, wg, wu, own_down, dn, outbox, arr, hid, summed, ret, mixing, total,
    load_sem, zs, zr, xs, xr, fs, fr, ys, yr, cs, cr, hs, hr, bs, br,
):
    dp = lax.axis_index("dp")
    y, core = dp // 2, dp % 2
    e = lax.axis_index("expert")
    h = lax.axis_index("head")

    def z_peer(off):
        return {"expert": (e + off + 2 * NZ) % NZ}

    def x_peer(off):
        return {"head": (h + off + NX) % NX}

    def y_at(off):
        return (y + off + NY) % NY

    def y_dp(off):
        return y_at(off) * 2 + core

    sibling = y * 2 + (1 - core)

    loads = [
        pltpu.make_async_copy(routes, rts, load_sem.at[0]),
        pltpu.make_async_copy(route_weights, rtw, load_sem.at[1]),
        pltpu.make_async_copy(
            tokens.at[:, pl.ds(pl.multiple_of(h * QUARTER, QUARTER), QUARTER)], tok, load_sem.at[2]
        ),
        pltpu.make_async_copy(down.at[0], own_down, load_sem.at[3]),
    ]
    for r, off in enumerate((0, -1, 1, 2)):
        q = (h + off + NX) % NX
        src = pl.ds(pl.multiple_of(q * QUARTER, QUARTER), QUARTER)
        loads.append(pltpu.make_async_copy(gate.at[0, src], wg.at[r], load_sem.at[4 + 2 * r]))
        loads.append(pltpu.make_async_copy(up.at[0, src], wu.at[r], load_sem.at[5 + 2 * r]))
    for copy in loads:
        copy.start()

    bar = pltpu.get_barrier_semaphore()

    def greet(i, c):
        pl.semaphore_signal(bar, inc=1, device_id=z_peer(i), device_id_type=MESH)
        return c

    lax.fori_loop(1, NZ, greet, 0)
    for off in (1, -1, 2):
        pl.semaphore_signal(bar, inc=1, device_id=x_peer(off), device_id_type=MESH)
    for off in (1, -1, 2, -2):
        pl.semaphore_signal(bar, inc=1, device_id={"dp": y_dp(off)}, device_id_type=MESH)
    pl.semaphore_signal(bar, inc=1, device_id={"dp": sibling}, device_id_type=MESH)
    column = y // 2
    at_home = (column == h).astype(jnp.int32)
    for s in range(2):
        for p in range(NX):
            @pl.when((y != 2 * h + s) | (h != p))
            def _():
                pl.semaphore_signal(
                    bar, inc=1, device_id={"dp": (2 * h + s) * 2 + core, "head": p}, device_id_type=MESH
                )

    tok_rows = tok.shape[0]
    row = lax.broadcasted_iota(jnp.int32, (ROWS, tok_rows), 0)
    block = row >> 4
    slot = row & (CAP - 1)
    size = (block + 1) >> 1
    target = ((e + NZ + jnp.where((block & 1) == 1, size, -size)) & (NZ - 1)) * 8
    loads[0].wait()
    loads[1].wait()
    chosen = jnp.zeros((ROWS, tok_rows), jnp.float32)
    weight = jnp.zeros((ROWS, tok_rows), jnp.float32)
    for i in range(8):
        match = rts[i : i + 1, :] == target
        chosen = jnp.where(match, 1.0, chosen)
        weight = jnp.where(match, rtw[i : i + 1, :], weight)
    upto = (
        lax.broadcasted_iota(jnp.int32, (tok_rows, tok_rows), 0)
        <= lax.broadcasted_iota(jnp.int32, (tok_rows, tok_rows), 1)
    )
    count = jnp.dot(
        chosen.astype(jnp.bfloat16),
        jnp.where(upto, 1.0, 0.0).astype(jnp.bfloat16),
        preferred_element_type=jnp.float32,
    )
    picked = jnp.where(count == (slot + 1).astype(jnp.float32), chosen, 0.0)
    loads[2].wait()
    outbox[...] = jnp.dot(
        picked.astype(jnp.bfloat16), tok[...], preferred_element_type=jnp.float32
    ).astype(jnp.bfloat16)
    loads[3].wait()

    pl.semaphore_wait(bar, (NZ - 1) + 3 + 4 + 1 + NY - at_home)

    def frag_copy(i):
        return pltpu.make_async_remote_copy(
            src_ref=own_down.at[pl.ds(i * FRAG, FRAG)],
            dst_ref=dn.at[core, i, y % 2, h],
            send_sem=fs.at[i],
            recv_sem=fr.at[y % 2, h],
            device_id={"dp": i * 2 + core, "head": column},
            device_id_type=MESH,
        )

    def frag_arrived(s, p):
        pltpu.make_async_remote_copy(
            src_ref=own_down.at[pl.ds(0, FRAG)],
            dst_ref=dn.at[core, y, s, p],
            send_sem=fs.at[0],
            recv_sem=fr.at[s, p],
            device_id={"dp": (2 * h + s) * 2 + core, "head": p},
            device_id_type=MESH,
        ).wait_recv()

    def own_frag():
        return pltpu.make_async_copy(
            own_down.at[pl.ds(pl.multiple_of(y * FRAG, FRAG), FRAG)], dn.at[core, y, y % 2, h], load_sem.at[3]
        )

    def y_copy(block_off, to_off):
        there = y_index(block_off - to_off)
        return pltpu.make_async_remote_copy(
            src_ref=dn.at[core, y_at(block_off)],
            dst_ref=dn.at[core, y_at(block_off)],
            send_sem=ys.at[there],
            recv_sem=yr.at[there],
            device_id={"dp": y_dp(to_off)},
            device_id_type=MESH,
        )

    def y_arrived(off):
        pltpu.make_async_remote_copy(
            src_ref=dn.at[core, y_at(off)],
            dst_ref=dn.at[core, y_at(off)],
            send_sem=ys.at[y_index(off)],
            recv_sem=yr.at[y_index(off)],
            device_id={"dp": y_dp(1)},
            device_id_type=MESH,
        ).wait_recv()

    def core_copy(off):
        i = (off + NY) % NY
        return pltpu.make_async_remote_copy(
            src_ref=dn.at[core, y_at(off)],
            dst_ref=dn.at[core, y_at(off)],
            send_sem=cs.at[i],
            recv_sem=cr.at[i],
            device_id={"dp": sibling},
            device_id_type=MESH,
        )

    def core_arrived(off):
        i = (off + NY) % NY
        pltpu.make_async_remote_copy(
            src_ref=dn.at[1 - core, y_at(off)],
            dst_ref=dn.at[1 - core, y_at(off)],
            send_sem=cs.at[i],
            recv_sem=cr.at[i],
            device_id={"dp": sibling},
            device_id_type=MESH,
        ).wait_recv()

    def z_copy(k):
        return pltpu.make_async_remote_copy(
            src_ref=outbox.at[rows_of(k)],
            dst_ref=arr.at[0, rows_of(k)],
            send_sem=zs.at[k],
            recv_sem=zr.at[k],
            device_id=z_peer(offset_of(k)),
            device_id_type=MESH,
        )

    def x_copy(j, k):
        return pltpu.make_async_remote_copy(
            src_ref=arr.at[0, rows_of(k)],
            dst_ref=arr.at[j + 1, rows_of(k)],
            send_sem=xs.at[j, k],
            recv_sem=xr.at[j, k],
            device_id=x_peer(1 - 2 * j),
            device_id_type=MESH,
        )

    def far_copy(k):
        j = k % 2
        return pltpu.make_async_remote_copy(
            src_ref=arr.at[j + 1, rows_of(k)],
            dst_ref=arr.at[3, rows_of(k)],
            send_sem=xs.at[2, k],
            recv_sem=xr.at[2, k],
            device_id=x_peer(1 - 2 * j),
            device_id_type=MESH,
        )

    def back_copy(k):
        return pltpu.make_async_remote_copy(
            src_ref=summed.at[rows_of(k)],
            dst_ref=ret.at[rows_of(k)],
            send_sem=bs.at[k],
            recv_sem=br.at[k],
            device_id=z_peer(-offset_of(k)),
            device_id_type=MESH,
        )

    def loop(lo, hi, step):
        def run(k, c):
            step(k)
            return c

        lax.fori_loop(lo, hi, run, 0)

    def direct_copy(k):
        return pltpu.make_async_remote_copy(
            src_ref=arr.at[0, rows_of(k)],
            dst_ref=arr.at[3, rows_of(k)],
            send_sem=xs.at[2, k],
            recv_sem=xr.at[2, k],
            device_id=x_peer(2),
            device_id_type=MESH,
        )

    def spread(k):
        x_copy(0, k).start()
        x_copy(1, k).start()

    def forward(k):
        x_copy(k % 2, k).wait_recv()
        far_copy(k).start()

    def pass_on(k):
        z_copy(k).wait_recv()
        spread(k)

    for i in range(NY):
        @pl.when((column != h) | (y != i))
        def _():
            frag_copy(i).start()

    @pl.when(column == h)
    def _():
        own_frag().start()

    loop(1, NZ, lambda k: z_copy(k).start())
    arr[0, :CAP, :] = outbox[:CAP, :]
    spread(0)

    mix = (picked * weight).T
    mix_high = mix.astype(jnp.bfloat16)
    mixing[0] = mix_high
    mixing[1] = (mix - mix_high.astype(jnp.float32)).astype(jnp.bfloat16)

    def expert_front(g):
        first, last = GROUPS[g]
        n = (last - first) * CAP
        rows = slice(first * CAP, last * CAP)
        gate_act = jnp.zeros((n, wg.shape[2]), jnp.float32)
        up_act = jnp.zeros((n, wg.shape[2]), jnp.float32)
        for r in range(NX):
            if r == 1:
                loop(first, last, lambda k: x_copy(1 - k % 2, k).wait_recv())
                loop(max(first, DIRECT), last, lambda k: x_copy(k % 2, k).wait_recv())
            if r == 3:
                loop(first, last, lambda k: far_copy(k).wait_recv())
            a = arr[r, rows, :]
            gate_act += jnp.dot(a, wg[r], preferred_element_type=jnp.float32)
            up_act += jnp.dot(a, wu[r], preferred_element_type=jnp.float32)
        hidden = gate_act / (1.0 + jnp.exp(-gate_act)) * up_act
        hid[h, rows, :] = hidden.astype(jnp.bfloat16)
        for j in range(3):
            hid_copy(g, j).start()

    def hid_copy(g, j):
        first, last = GROUPS[g]
        rows = pl.ds(first * CAP, (last - first) * CAP)
        return pltpu.make_async_remote_copy(
            src_ref=hid.at[h, rows],
            dst_ref=hid.at[h, rows],
            send_sem=hs.at[g, j],
            recv_sem=hr.at[g, j],
            device_id=x_peer((1, -1, 2)[j]),
            device_id_type=MESH,
        )

    def hid_arrived(g, j):
        first, last = GROUPS[g]
        rows = pl.ds(first * CAP, (last - first) * CAP)
        off = (1, -1, 2)[j]
        source = (h - off + NX) % NX
        pltpu.make_async_remote_copy(
            src_ref=hid.at[source, rows],
            dst_ref=hid.at[source, rows],
            send_sem=hs.at[g, j],
            recv_sem=hr.at[g, j],
            device_id=x_peer(off),
            device_id_type=MESH,
        ).wait_recv()

    def expert_back(g):
        first, last = GROUPS[g]
        rows = slice(first * CAP, last * CAP)
        for j in range(3):
            hid_arrived(g, j)
        for s in range(2):
            for c in range(2):
                value = sum(
                    jnp.dot(
                        hid[p, rows, :],
                        dn[c, :, s, p].reshape(NY * FRAG, dn.shape[-1]),
                        preferred_element_type=jnp.float32,
                    )
                    for p in range(NX)
                )
                b = 2 * s + c
                summed[rows, b * 256 : (b + 1) * 256] = value.astype(jnp.bfloat16)
        loop(max(first, 1), last, lambda k: back_copy(k).start())

    def pass_far(k):
        pass_on(k)
        direct_copy(k).start()

    loop(1, 3, pass_on)
    for s in range(2):
        for p in range(NX):
            @pl.when((y != 2 * h + s) | (h != p))
            def _():
                frag_arrived(s, p)

    @pl.when(column == h)
    def _():
        own_frag().wait()

    y_first = [y_copy(0, off) for off in (2, -2, 1, -1)]
    for copy in y_first:
        copy.start()
    core_copy(0).start()
    loop(3, 5, pass_on)
    forward(0)
    loop(5, 7, pass_on)
    loop(1, 3, forward)
    for copy in loads[4:]:
        copy.wait()
    loop(7, 9, pass_on)
    loop(3, 5, forward)
    loop(9, 11, pass_on)
    loop(5, 7, forward)
    expert_front(0)
    y_arrived(-2)
    y_arrived(2)
    y_second = [y_copy(-2, 2), y_copy(-2, 1), y_copy(2, -1)]
    for copy in y_second:
        copy.start()
    loop(11, 13, pass_on)
    loop(7, 9, forward)
    y_arrived(-1)
    y_arrived(1)
    for off in (-1, 1, -2, 2):
        core_copy(off).start()
    loop(13, 15, pass_far)
    loop(9, 11, forward)
    expert_front(1)
    loop(11, 13, forward)
    pass_far(15)
    expert_front(2)
    for off in (-3, 3, 4):
        y_arrived(off)
        core_copy(off).start()
    expert_front(3)
    for i in range(NY):
        core_arrived(i)
    expert_back(2)
    expert_back(3)
    expert_back(1)
    expert_back(0)
    ret[:CAP, :] = summed[:CAP, :]

    for i in range(NY):
        @pl.when((column != h) | (y != i))
        def _():
            frag_copy(i).wait_send()
    loop(1, NZ, lambda k: z_copy(k).wait_send())
    for j in range(2):
        loop(0, NZ, lambda k: x_copy(j, k).wait_send())
    loop(0, DIRECT, lambda k: far_copy(k).wait_send())
    loop(DIRECT, NZ, lambda k: direct_copy(k).wait_send())
    for copy in y_first + y_second:
        copy.wait_send()
    for i in range(NY):
        core_copy(i).wait_send()
    for g in range(len(GROUPS)):
        for j in range(3):
            hid_copy(g, j).wait_send()

    def mixed(lo, hi):
        rows = slice(lo * CAP, hi * CAP)
        return sum(
            jnp.dot(mixing[i, :, rows], ret[rows, :], preferred_element_type=jnp.float32) for i in range(2)
        )

    half = NZ // 2
    loop(half, NZ, lambda k: back_copy(k).wait_recv())
    total[...] = mixed(half, NZ)
    loop(1, half, lambda k: back_copy(k).wait_recv())
    out[...] = (total[...] + mixed(0, half)).astype(jnp.bfloat16)
    loop(1, NZ, lambda k: back_copy(k).wait_send())


def body(tokens, routes, route_weights, gate_weight, up_weight, down_weight):
    tok_rows = tokens.shape[0]
    hidden = gate_weight.shape[2]
    bf16, f32 = jnp.bfloat16, jnp.float32
    dma = pltpu.SemaphoreType.DMA
    groups = len(GROUPS)
    return pl.pallas_call(
        kernel,
        out_shape=jax.ShapeDtypeStruct((tok_rows, QUARTER), bf16),
        in_specs=[pl.BlockSpec(memory_space=pltpu.HBM)] * 6,
        out_specs=pl.BlockSpec(memory_space=pltpu.VMEM),
        scratch_shapes=[
            pltpu.VMEM((tok_rows, QUARTER), bf16),
            pltpu.VMEM((8, tok_rows), jnp.int32),
            pltpu.VMEM((8, tok_rows), f32),
            pltpu.VMEM((NX, QUARTER, hidden), bf16),
            pltpu.VMEM((NX, QUARTER, hidden), bf16),
            pltpu.VMEM((hidden, 256), bf16),
            pltpu.VMEM((2, NY, 2, NX, FRAG, 256), bf16),
            pltpu.VMEM((ROWS, QUARTER), bf16),
            pltpu.VMEM((NX, ROWS, QUARTER), bf16),
            pltpu.VMEM((NX, ROWS, hidden), bf16),
            pltpu.VMEM((ROWS, QUARTER), bf16),
            pltpu.VMEM((ROWS, QUARTER), bf16),
            pltpu.VMEM((2, tok_rows, ROWS), bf16),
            pltpu.VMEM((tok_rows, QUARTER), f32),
            dma((12,)),
            dma((NZ,)), dma((NZ,)),
            dma((3, NZ)), dma((3, NZ)),
            dma((NY,)), dma((2, NX)),
            dma((7,)), dma((7,)),
            dma((NY,)), dma((NY,)),
            dma((groups, 3)), dma((groups, 3)),
            dma((NZ,)), dma((NZ,)),
        ],
        compiler_params=pltpu.CompilerParams(
            collective_id=0, has_side_effects=True, vmem_limit_bytes=62 * 2**20
        ),
        cost_estimate=pl.CostEstimate(
            flops=2 * ROWS * hidden * 3 * 4096, bytes_accessed=6 * 2**20, transcendentals=ROWS * hidden
        ),
    )(tokens, routes.T, route_weights.T, gate_weight, up_weight, down_weight)


def solution(mesh):
    return jax.shard_map(
        body,
        mesh=mesh,
        in_specs=(
            P(("dp", "expert"), None),
            P(("dp", "expert"), None),
            P(("dp", "expert"), None),
            P("expert", None, "head"),
            P("expert", None, "head"),
            P("expert", "head", "dp"),
        ),
        out_specs=P(("dp", "expert"), "head"),
        check_vma=False,
    )
```

time: 101 us -> 90.3 us (0.89); the launches traced: 101 us -> 88.8 us
  local copies, waits for them, and re-layouts: 7.58 us -> 1.67 us
  Pallas kernels: 93.1 us -> 87.2 us
    pallas_call x1, Pallas kernels: 93.1 us -> 87.2 us  [body(): pl.pallas_call(kernel, out_shape=jax.ShapeDtypeStruct((tok_rows, QUARTER)...]
    unnamed x11 -> x1, local copies, waits for them, and re-layouts: 7.58 us -> 1.67 us
where the time goes in v2:
time: 90.3 us; the launch traced here: 88.8 us
  Pallas kernels  87.2 us (97%)
  local copies, waits for them, and re-layouts  1.67 us (2%)
    pallas_call x1, Pallas kernels, body(): pl.pallas_call(kernel, out_shape=jax.ShapeDtypeStruct((tok_rows, QUARTER)...  87.2 us

profile of v2, /device:TPU:1, one launch (start us, length us, event | category | flops | bytes accessed | tf_op | source)
XLA Modules:
  0.0 88.8 jit_solution(13206615227503457485)
XLA Ops:
  0.0 87.2 %shard_map.64 = bf16[128,1024]{1,0:T(8,128)(2,1)} custom-call(bf16[128,4096]{1,0:T(8,128)(2,1)} %tokens.1, s32[8,128]{1,0:T(8,128)} %bitcast.2, f32[8,128]{1,0:T(8,128)} %bitcast.3, bf16[1,4096,256]{2,1,0:T(8,128)(2,1)} %gate.1, bf16[1,4096,256]{2,1,0:T(8,128)(2,1)} %up.1, bf16[1,256,256]{2,1,0:T(8,128)(2,1)} %down.1), custom_call_target="tpu_custom_call" | custom-call | flops 1610612736 | bytes 6291456 | tf_op jit(solution)/shard_map/pallas_call | solution.py:445
  87.2 1.7 %copy.8 = bf16[128,1024]{1,0:T(8,128)(2,1)} copy(bf16[128,1024]{1,0:T(8,128)(2,1)} %shard_map.64) | data formatting | bytes 524288

commit v3 on v2

--- a/solution.py
+++ b/solution.py
@@ -13,13 +13,12 @@
 QUARTER = 1024
 ROWS = NZ * CAP
 FRAG = 32
-DIRECT = 13
-GROUPS = ((0, 5), (5, 9), (9, 13), (13, 16))
+GROUPS = ((0, 5), (5, 11), (11, 16))
 Y_OFFSETS = (1, -1, 2, -2, 3, -3, 4)
 
 
 def offset_of(k):
-    return (k + 1) // 2 * (2 * (k % 2) - 1)
+    return (8 - (k + 1) // 2) * (2 * (k % 2) - 1)
 
 
 def y_index(off):
@@ -68,9 +67,6 @@
         src = pl.ds(pl.multiple_of(q * QUARTER, QUARTER), QUARTER)
         loads.append(pltpu.make_async_copy(gate.at[0, src], wg.at[r], load_sem.at[4 + 2 * r]))
         loads.append(pltpu.make_async_copy(up.at[0, src], wu.at[r], load_sem.at[5 + 2 * r]))
-    for copy in loads:
-        copy.start()
-
     bar = pltpu.get_barrier_semaphore()
 
     def greet(i, c):
@@ -93,11 +89,14 @@
                     bar, inc=1, device_id={"dp": (2 * h + s) * 2 + core, "head": p}, device_id_type=MESH
                 )
 
+    for copy in loads:
+        copy.start()
+
     tok_rows = tok.shape[0]
     row = lax.broadcasted_iota(jnp.int32, (ROWS, tok_rows), 0)
     block = row >> 4
     slot = row & (CAP - 1)
-    size = (block + 1) >> 1
+    size = 8 - ((block + 1) >> 1)
     target = ((e + NZ + jnp.where((block & 1) == 1, size, -size)) & (NZ - 1)) * 8
     loads[0].wait()
     loads[1].wait()
@@ -209,18 +208,7 @@
             dst_ref=arr.at[j + 1, rows_of(k)],
             send_sem=xs.at[j, k],
             recv_sem=xr.at[j, k],
-            device_id=x_peer(1 - 2 * j),
-            device_id_type=MESH,
-        )
-
-    def far_copy(k):
-        j = k % 2
-        return pltpu.make_async_remote_copy(
-            src_ref=arr.at[j + 1, rows_of(k)],
-            dst_ref=arr.at[3, rows_of(k)],
-            send_sem=xs.at[2, k],
-            recv_sem=xr.at[2, k],
-            device_id=x_peer(1 - 2 * j),
+            device_id=x_peer((1, -1, 2)[j]),
             device_id_type=MESH,
         )
 
@@ -241,23 +229,9 @@
 
         lax.fori_loop(lo, hi, run, 0)
 
-    def direct_copy(k):
-        return pltpu.make_async_remote_copy(
-            src_ref=arr.at[0, rows_of(k)],
-            dst_ref=arr.at[3, rows_of(k)],
-            send_sem=xs.at[2, k],
-            recv_sem=xr.at[2, k],
-            device_id=x_peer(2),
-            device_id_type=MESH,
-        )
-
     def spread(k):
-        x_copy(0, k).start()
-        x_copy(1, k).start()
-
-    def forward(k):
-        x_copy(k % 2, k).wait_recv()
-        far_copy(k).start()
+        for j in range(3):
+            x_copy(j, k).start()
 
     def pass_on(k):
         z_copy(k).wait_recv()
@@ -272,9 +246,9 @@
     def _():
         own_frag().start()
 
-    loop(1, NZ, lambda k: z_copy(k).start())
-    arr[0, :CAP, :] = outbox[:CAP, :]
-    spread(0)
+    loop(0, NZ - 1, lambda k: z_copy(k).start())
+    arr[0, -CAP:, :] = outbox[-CAP:, :]
+    spread(NZ - 1)
 
     mix = (picked * weight).T
     mix_high = mix.astype(jnp.bfloat16)
@@ -288,11 +262,8 @@
         gate_act = jnp.zeros((n, wg.shape[2]), jnp.float32)
         up_act = jnp.zeros((n, wg.shape[2]), jnp.float32)
         for r in range(NX):
-            if r == 1:
-                loop(first, last, lambda k: x_copy(1 - k % 2, k).wait_recv())
-                loop(max(first, DIRECT), last, lambda k: x_copy(k % 2, k).wait_recv())
-            if r == 3:
-                loop(first, last, lambda k: far_copy(k).wait_recv())
+            if r:
+                loop(first, last, lambda k: x_copy(r - 1, k).wait_recv())
             a = arr[r, rows, :]
             gate_act += jnp.dot(a, wg[r], preferred_element_type=jnp.float32)
             up_act += jnp.dot(a, wu[r], preferred_element_type=jnp.float32)
@@ -327,11 +298,12 @@
             device_id_type=MESH,
         ).wait_recv()
 
-    def expert_back(g):
-        first, last = GROUPS[g]
+    def expert_back(groups):
+        first, last = GROUPS[groups[0]][0], GROUPS[groups[-1]][1]
         rows = slice(first * CAP, last * CAP)
-        for j in range(3):
-            hid_arrived(g, j)
+        for g in groups:
+            for j in range(3):
+                hid_arrived(g, j)
         for s in range(2):
             for c in range(2):
                 value = sum(
@@ -344,13 +316,8 @@
                 )
                 b = 2 * s + c
                 summed[rows, b * 256 : (b + 1) * 256] = value.astype(jnp.bfloat16)
-        loop(max(first, 1), last, lambda k: back_copy(k).start())
-
-    def pass_far(k):
-        pass_on(k)
-        direct_copy(k).start()
-
-    loop(1, 3, pass_on)
+        loop(first, min(last, NZ - 1), lambda k: back_copy(k).start())
+
     for s in range(2):
         for p in range(NX):
             @pl.when((y != 2 * h + s) | (h != p))
@@ -365,55 +332,42 @@
     for copy in y_first:
         copy.start()
     core_copy(0).start()
-    loop(3, 5, pass_on)
-    forward(0)
-    loop(5, 7, pass_on)
-    loop(1, 3, forward)
     for copy in loads[4:]:
         copy.wait()
-    loop(7, 9, pass_on)
-    loop(3, 5, forward)
-    loop(9, 11, pass_on)
-    loop(5, 7, forward)
-    expert_front(0)
+    loop(0, 3, pass_on)
     y_arrived(-2)
     y_arrived(2)
     y_second = [y_copy(-2, 2), y_copy(-2, 1), y_copy(2, -1)]
     for copy in y_second:
         copy.start()
-    loop(11, 13, pass_on)
-    loop(7, 9, forward)
+    loop(3, 5, pass_on)
     y_arrived(-1)
     y_arrived(1)
     for off in (-1, 1, -2, 2):
         core_copy(off).start()
-    loop(13, 15, pass_far)
-    loop(9, 11, forward)
-    expert_front(1)
-    loop(11, 13, forward)
-    pass_far(15)
-    expert_front(2)
+    loop(5, 7, pass_on)
+    expert_front(0)
     for off in (-3, 3, 4):
         y_arrived(off)
         core_copy(off).start()
-    expert_front(3)
+    loop(7, 11, pass_on)
     for i in range(NY):
         core_arrived(i)
-    expert_back(2)
-    expert_back(3)
-    expert_back(1)
-    expert_back(0)
-    ret[:CAP, :] = summed[:CAP, :]
+    expert_back((0,))
+    expert_front(1)
+    loop(11, NZ - 1, pass_on)
+    expert_back((1,))
+    expert_front(2)
+    expert_back((2,))
+    ret[-CAP:, :] = summed[-CAP:, :]
 
     for i in range(NY):
         @pl.when((column != h) | (y != i))
         def _():
             frag_copy(i).wait_send()
-    loop(1, NZ, lambda k: z_copy(k).wait_send())
-    for j in range(2):
+    loop(0, NZ - 1, lambda k: z_copy(k).wait_send())
+    for j in range(3):
         loop(0, NZ, lambda k: x_copy(j, k).wait_send())
-    loop(0, DIRECT, lambda k: far_copy(k).wait_send())
-    loop(DIRECT, NZ, lambda k: direct_copy(k).wait_send())
     for copy in y_first + y_second:
         copy.wait_send()
     for i in range(NY):
@@ -429,11 +383,11 @@
         )
 
     half = NZ // 2
-    loop(half, NZ, lambda k: back_copy(k).wait_recv())
-    total[...] = mixed(half, NZ)
-    loop(1, half, lambda k: back_copy(k).wait_recv())
-    out[...] = (total[...] + mixed(0, half)).astype(jnp.bfloat16)
-    loop(1, NZ, lambda k: back_copy(k).wait_send())
+    loop(0, half, lambda k: back_copy(k).wait_recv())
+    total[...] = mixed(0, half)
+    loop(half, NZ - 1, lambda k: back_copy(k).wait_recv())
+    out[...] = (total[...] + mixed(half, NZ)).astype(jnp.bfloat16)
+    loop(0, NZ - 1, lambda k: back_copy(k).wait_send())
 
 
 def body(tokens, routes, route_weights, gate_weight, up_weight, down_weight):

time: 90.3 us -> 80.5 us (0.89); the launches traced: 88.8 us -> 80.3 us
  Pallas kernels: 87.2 us -> 78.6 us
    pallas_call x1, Pallas kernels: 87.2 us -> 78.6 us  [body(): pl.pallas_call(kernel, out_shape=jax.ShapeDtypeStruct((tok_rows, QUARTER)...]
where the time goes in v3:
time: 80.5 us; the launch traced here: 80.3 us
  Pallas kernels  78.6 us (98%)
  local copies, waits for them, and re-layouts  1.67 us (2%)
    pallas_call x1, Pallas kernels, body(): pl.pallas_call(kernel, out_shape=jax.ShapeDtypeStruct((tok_rows, QUARTER)...  78.6 us
    unnamed x1, local copies, waits for them, and re-layouts  1.67 us

profile of v3, /device:TPU:1, one launch (start us, length us, event | category | flops | bytes accessed | tf_op | source)
XLA Modules:
  0.0 80.3 jit_solution(10571447276170801356)
XLA Ops:
  0.0 78.6 %shard_map.64 = bf16[128,1024]{1,0:T(8,128)(2,1)} custom-call(bf16[128,4096]{1,0:T(8,128)(2,1)} %tokens.1, s32[8,128]{1,0:T(8,128)} %bitcast.2, f32[8,128]{1,0:T(8,128)} %bitcast.3, bf16[1,4096,256]{2,1,0:T(8,128)(2,1)} %gate.1, bf16[1,4096,256]{2,1,0:T(8,128)(2,1)} %up.1, bf16[1,256,256]{2,1,0:T(8,128)(2,1)} %down.1), custom_call_target="tpu_custom_call" | custom-call | flops 1610612736 | bytes 6291456 | tf_op jit(solution)/shard_map/pallas_call | solution.py:399
  78.6 1.7 %copy.8 = bf16[128,1024]{1,0:T(8,128)(2,1)} copy(bf16[128,1024]{1,0:T(8,128)(2,1)} %shard_map.64) | data formatting | bytes 524288

commit v4 on v3

--- a/solution.py
+++ b/solution.py
@@ -13,6 +13,7 @@
 QUARTER = 1024
 ROWS = NZ * CAP
 FRAG = 32
+EARLY = 13
 GROUPS = ((0, 5), (5, 11), (11, 16))
 Y_OFFSETS = (1, -1, 2, -2, 3, -3, 4)
 
@@ -246,14 +247,15 @@
     def _():
         own_frag().start()
 
-    loop(0, NZ - 1, lambda k: z_copy(k).start())
+    loop(EARLY, NZ - 1, lambda k: z_copy(k).start())
+    loop(0, EARLY, lambda k: z_copy(k).start())
     arr[0, -CAP:, :] = outbox[-CAP:, :]
     spread(NZ - 1)
 
     mix = (picked * weight).T
     mix_high = mix.astype(jnp.bfloat16)
-    mixing[0] = mix_high
-    mixing[1] = (mix - mix_high.astype(jnp.float32)).astype(jnp.bfloat16)
+    mixing[: tok.shape[0]] = mix_high
+    mixing[tok.shape[0] :] = (mix - mix_high.astype(jnp.float32)).astype(jnp.bfloat16)
 
     def expert_front(g):
         first, last = GROUPS[g]
@@ -332,6 +334,7 @@
     for copy in y_first:
         copy.start()
     core_copy(0).start()
+    loop(EARLY, NZ - 1, pass_on)
     for copy in loads[4:]:
         copy.wait()
     loop(0, 3, pass_on)
@@ -355,7 +358,7 @@
         core_arrived(i)
     expert_back((0,))
     expert_front(1)
-    loop(11, NZ - 1, pass_on)
+    loop(11, EARLY, pass_on)
     expert_back((1,))
     expert_front(2)
     expert_back((2,))
@@ -378,15 +381,14 @@
 
     def mixed(lo, hi):
         rows = slice(lo * CAP, hi * CAP)
-        return sum(
-            jnp.dot(mixing[i, :, rows], ret[rows, :], preferred_element_type=jnp.float32) for i in range(2)
-        )
-
-    half = NZ // 2
-    loop(0, half, lambda k: back_copy(k).wait_recv())
-    total[...] = mixed(0, half)
-    loop(half, NZ - 1, lambda k: back_copy(k).wait_recv())
-    out[...] = (total[...] + mixed(half, NZ)).astype(jnp.bfloat16)
+        both = jnp.dot(mixing[:, rows], ret[rows, :], preferred_element_type=jnp.float32)
+        return both[: tok.shape[0]] + both[tok.shape[0] :]
+
+    cut = 8
+    loop(0, cut, lambda k: back_copy(k).wait_recv())
+    total[...] = mixed(0, cut)
+    loop(cut, NZ - 1, lambda k: back_copy(k).wait_recv())
+    out[...] = (total[...] + mixed(cut, NZ)).astype(jnp.bfloat16)
     loop(0, NZ - 1, lambda k: back_copy(k).wait_send())
 
 
@@ -414,7 +416,7 @@
             pltpu.VMEM((NX, ROWS, hidden), bf16),
             pltpu.VMEM((ROWS, QUARTER), bf16),
             pltpu.VMEM((ROWS, QUARTER), bf16),
-            pltpu.VMEM((2, tok_rows, ROWS), bf16),
+            pltpu.VMEM((2 * tok_rows, ROWS), bf16),
             pltpu.VMEM((tok_rows, QUARTER), f32),
             dma((12,)),
             dma((NZ,)), dma((NZ,)),

time: 80.5 us -> 80.4 us (level)
  no operation moved by 1% of the time
where the time goes in v4:
time: 80.4 us; the launch traced here: 79.9 us
  Pallas kernels  78.2 us (97%)
  local copies, waits for them, and re-layouts  1.67 us (2%)
    pallas_call x1, Pallas kernels, body(): pl.pallas_call(kernel, out_shape=jax.ShapeDtypeStruct((tok_rows, QUARTER)...  78.2 us
    unnamed x1, local copies, waits for them, and re-layouts  1.67 us

profile of v4, /device:TPU:1, one launch (start us, length us, event | category | flops | bytes accessed | tf_op | source)
XLA Modules:
  0.0 79.9 jit_solution(11308437746626777358)
XLA Ops:
  0.0 78.2 %shard_map.64 = bf16[128,1024]{1,0:T(8,128)(2,1)} custom-call(bf16[128,4096]{1,0:T(8,128)(2,1)} %tokens.1, s32[8,128]{1,0:T(8,128)} %bitcast.2, f32[8,128]{1,0:T(8,128)} %bitcast.3, bf16[1,4096,256]{2,1,0:T(8,128)(2,1)} %gate.1, bf16[1,4096,256]{2,1,0:T(8,128)(2,1)} %up.1, bf16[1,256,256]{2,1,0:T(8,128)(2,1)} %down.1), custom_call_target="tpu_custom_call" | custom-call | flops 1610612736 | bytes 6291456 | tf_op jit(solution)/shard_map/pallas_call | solution.py:401
  78.2 1.7 %copy.8 = bf16[128,1024]{1,0:T(8,128)(2,1)} copy(bf16[128,1024]{1,0:T(8,128)(2,1)} %shard_map.64) | data formatting | bytes 524288
